TPU v7x, 128 devices: a whole 4x4x4 slice. The times are simulated.
128 devices in a mesh: ctx: 8 (over x, core), head: 16 (over z, y).
Axes of the slice: x: 4, y: 4, z: 4, core: 2. Of those that a mesh axis runs over, the one named last changes fastest.
Arguments:
- features: bfloat16 [2048, 6144], P('ctx', 'head'), may hold values from -6 to 6
- w_query: bfloat16 [6144, 8192], P(None, 'head'), may hold values from -0.078125 to 0.078125
- w_key: bfloat16 [6144, 8192], P(None, 'head'), may hold values from -0.078125 to 0.078125
- w_value: bfloat16 [6144, 8192], P(None, 'head'), may hold values from -0.078125 to 0.078125
- log_decay: float32 [64, 2048], P('head', 'ctx'), may hold values from -1 to 0, as said below
- d_out: bfloat16 [2048, 8192], P('ctx', 'head'), may hold values from -0.011962891 to 0.011962891
Outputs:
- d_features: bfloat16 [2048, 6144], P(('ctx', 'head'))
Inputs may be any that keep to these rules, and one draw needn't show every extreme that they name: `log_decay`: entries are negative or zero.
All inputs are finite; a program needn't handle non-finite values.
Results may differ from a plain program's by a relative error of at most 0.023.
Values may be sent and summed in bfloat16 or wider, within the bound.
No kernel may reach another device: no remote copies, remote signals or barrier semaphores. Data moves between devices by JAX's collectives and lax.ppermute only.
A program may use at most 128 MiB of HBM per device.

v0:
```python
import jax
import jax.numpy as jnp
from jax import lax
from jax.sharding import PartitionSpec as P

HI = lax.Precision.HIGHEST


def prefix(shard, axis, combine, identity, reverse):
    count, index = (lax.axis_size(axis), lax.axis_index(axis))
    everything = jax.tree.map(
        lambda part, kind: lax.all_gather(part.astype(kind), axis),
        shard,
        (jnp.bfloat16, jnp.bfloat16),
    )
    start = jax.tree.map(
        lambda part, zero: jnp.broadcast_to(jnp.asarray(zero, part.dtype), part.shape),
        shard,
        identity,
    )

    def lap(k, before):
        at = count - 1 - k if reverse else k
        reached = at > index if reverse else at < index
        new = combine(
            before, jax.tree.map(lambda part, own: part[at].astype(own.dtype), everything, shard)
        )
        return jax.tree.map(lambda a, b: jnp.where(reached, a, b), new, before)

    return lax.fori_loop(0, count, lap, start)


def split_heads(flat, head_count):
    return flat.reshape(flat.shape[0], head_count, -1).transpose(1, 0, 2)


def merge_heads(stacked):
    return stacked.transpose(1, 0, 2).reshape(stacked.shape[1], -1)


def forward_combine(earlier, later):
    return (earlier[0] + later[0], jnp.exp(later[0])[:, None, None] * earlier[1] + later[1])


def backward_combine(earlier, later):
    return (later[0] + earlier[0], later[1] + jnp.exp(later[0])[:, None, None] * earlier[1])


def shards(features, w_query, w_key, w_value, log_decay, d_out):
    f32 = jnp.float32
    row_count = features.shape[0]
    head_count = log_decay.shape[0]
    column_piece = lax.all_gather(features, "head", axis=1, tiled=True)
    query_sum = jnp.dot(column_piece, w_query, preferred_element_type=f32)
    key_sum = jnp.dot(column_piece, w_key, preferred_element_type=f32)
    value_sum = jnp.dot(column_piece, w_value, preferred_element_type=f32)
    queries = split_heads(query_sum.astype(jnp.bfloat16), head_count)
    keys_local = split_heads(key_sum.astype(jnp.bfloat16), head_count)
    values_local = split_heads(value_sum.astype(jnp.bfloat16), head_count)
    grads_out = split_heads(d_out, head_count)
    cumul = jnp.cumsum(log_decay, axis=1)
    total = cumul[:, -1]
    causal = jnp.tril(jnp.ones((row_count, row_count), dtype=bool))
    differ = cumul[:, :, None] - cumul[:, None, :]
    weights = jnp.where(causal[None], jnp.exp(jnp.minimum(differ, 0.0)), 0.0)
    tail = jnp.exp(total[:, None] - cumul)
    leading = jnp.exp(cumul)
    local_state = jnp.einsum(
        "hsi,hsj->hij",
        keys_local.astype(f32) * tail[:, :, None],
        values_local.astype(f32),
        precision=HI,
    )
    local_grad = jnp.einsum(
        "hti,htj->hij",
        queries.astype(f32) * leading[:, :, None],
        grads_out.astype(f32),
        precision=HI,
    )
    zero_total = jnp.zeros_like(total)
    zero_state = jnp.zeros_like(local_state)
    prefix_unused, state_in = prefix(
        (total, local_state), "ctx", forward_combine, (zero_total, zero_state), False
    )
    suffix_unused, grad_in = prefix(
        (total, local_grad), "ctx", backward_combine, (zero_total, zero_state), True
    )
    state_low = state_in.astype(jnp.bfloat16)
    grad_low = grad_in.astype(jnp.bfloat16)
    scores = (
        jnp.einsum("hti,hsi->hts", queries, keys_local, preferred_element_type=f32) * weights
    ).astype(jnp.bfloat16)
    mixing = (
        jnp.einsum("htj,hsj->hts", grads_out, values_local, preferred_element_type=f32) * weights
    ).astype(jnp.bfloat16)
    grad_query = jnp.einsum("hts,hsi->hti", mixing, keys_local, preferred_element_type=f32)
    grad_query = grad_query + leading[:, :, None] * jnp.einsum(
        "htj,hij->hti", grads_out, state_low, preferred_element_type=f32
    )
    grad_key = jnp.einsum("hts,hti->hsi", mixing, queries, preferred_element_type=f32)
    grad_key = grad_key + tail[:, :, None] * jnp.einsum(
        "hsj,hij->hsi", values_local, grad_low, preferred_element_type=f32
    )
    grad_value = jnp.einsum("hts,htj->hsj", scores, grads_out, preferred_element_type=f32)
    grad_value = grad_value + tail[:, :, None] * jnp.einsum(
        "hsi,hij->hsj", keys_local, grad_low, preferred_element_type=f32
    )
    query_grad_flat = merge_heads(grad_query.astype(jnp.bfloat16))
    key_grad_flat = merge_heads(grad_key.astype(jnp.bfloat16))
    value_grad_flat = merge_heads(grad_value.astype(jnp.bfloat16))
    summed = jnp.einsum("tc,dc->td", query_grad_flat, w_query, preferred_element_type=f32)
    summed = summed + jnp.einsum("tc,dc->td", key_grad_flat, w_key, preferred_element_type=f32)
    return lax.psum_scatter(
        (
            summed + jnp.einsum("tc,dc->td", value_grad_flat, w_value, preferred_element_type=f32)
        ).astype(jnp.bfloat16),
        "head",
        scatter_dimension=0,
        tiled=True,
    )


def solution(mesh):
    return jax.shard_map(
        shards,
        mesh=mesh,
        in_specs=(
            P("ctx", "head"),
            P(None, "head"),
            P(None, "head"),
            P(None, "head"),
            P("head", "ctx"),
            P("ctx", "head"),
        ),
        out_specs=P(("ctx", "head"), None),
        check_vma=False,
    )
```

profile of v0, /device:TPU:0, one launch (start us, length us, event | category | flops | bytes accessed | tf_op | source)
XLA Modules:
  0.0 224.2 jit_solution(17450735024143367338)
XLA Ops:
  6.5 0.0 all-gather.7.cloned.1.call-start
  6.5 0.7 all-gather.7.cloned.1.call-update
  7.3 0.0 all-gather.11.cloned.1.call-start
  7.3 0.7 reshape.133
  8.0 1.2 reduce-window.6
  9.2 0.1 slice.15
  9.3 0.1 copy.42
  9.5 0.1 copy.43
  9.6 0.1 add_bitcast_fusion
  9.6 0.1 slice.16
  9.7 0.1 copy.75
  9.8 1.2 dynamic-slice
  11.7 0.2 dynamic-update-slice
  12.0 14.7 %all-reduce = bf16[32]{0:T(256)(128)(2,1)S(1)} all-reduce(bf16[32]{0:T(256)(128)(2,1)S(1)} %dynamic-update-slice), channel_id=2, replica_groups=mesh['ctx'=8,'head'=16] {'ctx'}, use_global_device_ids=true, to_apply=%add | all-reduce | flops 32 | bytes 128
  26.7 0.1 reshape.142
  26.8 1.1 copy.70
  27.9 0.1 fusion.44
  28.0 36.8 %all-gather.7.cloned.1.call-done = bf16[256,6144]{1,0:T(8,128)(2,1)} async-done(((bf16[256,384]{1,0:T(8,128)(2,1)}), bf16[256,6144]{1,0:T(8,128)(2,1)}) %all-gather.7.cloned.1.call-update) | async-done | bytes 3145744 | tf_op jit(solution)/shard_map/all_gather | solution.py:53
  64.7 5.5 %fusion.17 = bf16[32,4,8,128]{3,2,1,0:T(8,128)(2,1)S(1)} fusion(bf16[256,6144]{1,0:T(8,128)(2,1)} %all-gather.7.cloned.1.call-done, bf16[6144,512]{1,0:T(8,128)(2,1)} %param.11), kind=kOutput, calls=%fused_computation.34 | convolution fusion | flops 1610743808 | bytes 9699328 | tf_op jit(solution)/shard_map/dot_general | solution.py:54
  70.2 1.4 convolution_convert_fusion.3
  71.7 0.0 all-gather.11.cloned.1.call-update
  71.7 0.0 all-gather.9.cloned.1.call-start
  71.8 0.0 copy-start
  71.8 5.7 %fusion.16 = bf16[32,4,8,128]{3,2,1,0:T(8,128)(2,1)S(1)} fusion(bf16[256,6144]{1,0:T(8,128)(2,1)} %all-gather.7.cloned.1.call-done, bf16[6144,512]{1,0:T(8,128)(2,1)} %param.12), kind=kOutput, calls=%fused_computation.33 | convolution fusion | flops 1610743808 | bytes 9699328 | tf_op jit(solution)/shard_map/dot_general | solution.py:55
  77.4 0.0 copy-done
  77.4 4.6 %fusion.15 = bf16[32,4,8,128]{3,2,1,0:T(8,128)(2,1)S(1)} fusion(bf16[256,6144]{1,0:T(8,128)(2,1)S(1)} %copy-done, bf16[6144,512]{1,0:T(8,128)(2,1)} %param.13), kind=kOutput, calls=%fused_computation.32 | convolution fusion | flops 1610743808 | bytes 9699328 | tf_op jit(solution)/shard_map/dot_general | solution.py:56
  82.1 1.5 convolution_convert_fusion.4
  83.5 0.4 fusion.5
  83.9 0.3 convolution_bitcast_fusion.6
  84.2 0.3 convolution_bitcast_fusion.4
  84.5 0.6 convolution_bitcast_fusion.2
  85.1 0.0 all-gather.9.cloned.1.call-update
  85.1 0.2 reduce-scatter.2.cloned.1.call-start
  85.3 9.1 %all-gather.11.cloned.1.call-done = bf16[32,128,128]{2,1,0:T(8,128)(2,1)} async-done(((bf16[4,128,128]{2,1,0:T(8,128)(2,1)}), bf16[32,128,128]{2,1,0:T(8,128)(2,1)}) %all-gather.11.cloned.1.call-update) | async-done | bytes 1048592 | tf_op jit(solution)/shard_map/all_gather | solution.py:12
  94.4 8.5 %while.31 = (s32[]{:T(128)}, f32[4,128,128]{2,1,0:T(8,128)S(1)}, s32[]{:T(128)}, bf16[8,4,128,128]{3,2,1,0:T(8,128)(2,1)}, bf16[8,4]{1,0:T(8,128)(2,1)S(1)}, /*index=5*/s32[]{:T(128)}, s32[]{:T(128)}, s32[]{:T(128)}, s32[]{:T(128)}) while((s32[]{:T(128)}, f32[4,128,128]{2,1,0:T(8,128)S(1)}, s32[]{:T(128)}, ...), condition=%wide.region_5.6_spmd.clone, body=%wide.region_4.5_spmd.clone.sunk | while | flops 327692 | bytes 655575 | solution.py:30
  94.4 1.0 fusion.67
  95.5 1.0 fusion.67
  96.6 1.0 fusion.67
  97.6 1.0 fusion.67
  98.7 1.0 fusion.67
  99.8 1.0 fusion.67
  100.8 1.0 fusion.67
  101.9 1.0 fusion.67
  102.9 16.5 %all-gather.9.cloned.1.call-done = bf16[32,128,128]{2,1,0:T(8,128)(2,1)} async-done(((bf16[4,128,128]{2,1,0:T(8,128)(2,1)}), bf16[32,128,128]{2,1,0:T(8,128)(2,1)}) %all-gather.9.cloned.1.call-update) | async-done | bytes 1048592 | tf_op jit(solution)/shard_map/all_gather | solution.py:12
  119.4 8.4 %while.30 = (s32[]{:T(128)}, f32[4,128,128]{2,1,0:T(8,128)S(1)}, s32[]{:T(128)}, bf16[8,4]{1,0:T(8,128)(2,1)S(1)}, bf16[8,4,128,128]{3,2,1,0:T(8,128)(2,1)}, /*index=5*/s32[]{:T(128)}, s32[]{:T(128)}) while((s32[]{:T(128)}, f32[4,128,128]{2,1,0:T(8,128)S(1)}, s32[]{:T(128)}, bf16[8,4]{1,0:T(8,128)(2,1)S(1)}, ...), condition=%wide.region_3.4_spmd.clone, body=%wide.region_2.3_spmd.clone.sunk | while | flops 327688 | bytes 655513 | solution.py:30
  119.4 1.0 fusion.66
  120.4 1.0 fusion.66
  121.5 1.0 fusion.66
  122.6 1.0 fusion.66
  123.6 1.0 fusion.66
  124.7 1.0 fusion.66
  125.7 1.0 fusion.66
  126.8 1.0 fusion.66
  127.8 0.3 fusion.12
  128.1 0.2 fusion.13
  128.3 0.0 slice-start
  128.3 0.2 fusion.14
  128.6 0.0 slice-start.1
  128.6 4.8 %fusion.45 = f32[256,6144]{1,0:T(8,128)S(1)} fusion(bf16[256,512]{0,1:T(8,128)(2,1)S(1)} %bitcast.157, bf16[6144,512]{1,0:T(8,128)(2,1)} %param.11), kind=kOutput, calls=%fused_computation.72 | convolution fusion | flops 1610612736 | bytes 12845056 | tf_op jit(solution)/shard_map/tc,dc->td/dot_general | solution.py:111
  133.4 0.0 slice-done
  133.4 1.9 convolution_add_fusion.1
  135.3 6.3 %fusion.2 = bf16[256,6144]{1,0:T(8,128)(2,1)} fusion(f32[256,6144]{1,0:T(8,128)S(1)} %convolution_add_fusion.1, bf16[256,512]{0,1:T(8,128)(2,1)S(1)} %bitcast.155, bf16[6144,512]{1,0:T(8,128)(2,1)} %param.13), kind=kOutput, calls=%fused_computation.8 | convolution fusion | flops 1613758464 | bytes 15990784 | tf_op jit(solution)/shard_map/tc,dc->td/dot_general | solution.py:115
  141.6 0.0 reduce-scatter.2.cloned.1.call-update
  141.6 76.0 %reduce-scatter.2.cloned.1.call-done = bf16[16,6144]{1,0:T(8,128)(2,1)} async-done(((bf16[256,6144]{1,0:T(8,128)(2,1)}), bf16[16,6144]{1,0:T(8,128)(2,1)}) %reduce-scatter.2.cloned.1.call-update) | async-done | bytes 196624 | tf_op jit(solution)/shard_map/reduce_scatter | solution.py:113
  (26 shorter events, 0.2 us)
Async XLA Ops:
  6.5 58.2 %all-gather.7.cloned.1.call-start = ((), (), s32[]{:S(2)}) async-start(), calls=%async_computation.1 | async-start | bytes 3342336 | tf_op jit(solution)/shard_map/all_gather | solution.py:53
  7.3 87.2 %all-gather.11.cloned.1.call-start = ((), (), s32[]{:S(2)}) async-start(), calls=%async_computation.4 | async-start | bytes 1179648 | tf_op jit(solution)/shard_map/all_gather | solution.py:12
  71.7 47.7 %all-gather.9.cloned.1.call-start = ((), (), s32[]{:S(2)}) async-start(), calls=%async_computation.3 | async-start | bytes 1179648 | tf_op jit(solution)/shard_map/all_gather | solution.py:12
  71.8 5.7 %copy-start = (bf16[256,6144]{1,0:T(8,128)(2,1)S(1)}, bf16[256,6144]{1,0:T(8,128)(2,1)}, u32[]{:S(2)}) copy-start(bf16[256,6144]{1,0:T(8,128)(2,1)} %all-gather.7.cloned.1.call-done) | copy-start | bytes 9437188
  85.1 132.6 %reduce-scatter.2.cloned.1.call-start = ((), (), s32[]{:S(2)}) async-start(), calls=%async_computation.2 | async-start | bytes 3342336 | tf_op jit(solution)/shard_map/reduce_scatter | solution.py:113
  128.3 5.1 %slice-start = ((s8[6291456]{0:T(1024)(128)(4,1)}), s8[4194304]{0:T(1024)(128)(4,1)S(1)}, s32[]{:S(2)}) async-start(s8[6291456]{0:T(1024)(128)(4,1)} %bitcast.153), calls=%async_computation.5 | async-start | bytes 8388608
  128.6 4.8 %slice-start.1 = ((s8[6291456]{0:T(1024)(128)(4,1)}), s8[2097152]{0:T(1024)(128)(4,1)S(1)}, s32[]{:S(2)}) async-start(s8[6291456]{0:T(1024)(128)(4,1)} %bitcast.153), calls=%async_computation.6 | async-start | bytes 4194304
Sparse Core Ops, SparseCore 0:
  9.5 55.1 all-gather.6
  71.8 22.5 all-gather.10
  96.1 23.1 all-gather.8
  141.8 75.8 reduce-scatter.1
where the time goes:
time: 225 us; the launch traced here: 224 us
  waiting for transfers between devices  139 us (62%)
  matrix products  33.9 us (15%)
  other arithmetic  17.8 us (8%)
  blocking collectives  14.7 us (7%)
  between operations  14 us (6%)
  local copies, waits for them, and re-layouts  3.84 us (2%)
    reduce_scatter x1, waiting for transfers between devices, shards(): lax.psum_scatter((summed + jnp.einsum('tc,dc->td', value_grad_flat, w_val...  76 us
    all_gather x1, waiting for transfers between devices, shards(): column_piece = lax.all_gather(features, 'head', axis=1, tiled=True)  36.8 us
    all_gather x2, waiting for transfers between devices, prefix(): lax.all_gather(part.astype(kind), axis)  25.6 us
    select_n x16, other arithmetic, lap(): return jax.tree.map(lambda a, b: jnp.where(reached, a, b), new, before)  16.2 us
    unnamed x1, blocking collectives  14.7 us
    dot_general x1, matrix products, shards(): jnp.einsum('tc,dc->td', value_grad_flat, w_value, preferred_element_type=...  6.29 us
    dot_general x1, matrix products, shards(): key_sum = jnp.dot(column_piece, w_key, preferred_element_type=f32)  5.67 us
    dot_general x1, matrix products, shards(): query_sum = jnp.dot(column_piece, w_query, preferred_element_type=f32)  5.52 us
  transfers between devices with their start and end apart: 4, of which 4 were waited for; matrix products, arithmetic and copies ran while one was open for 12% of the time, Pallas kernels for 0%

commit v1 on v0

--- a/solution.py
+++ b/solution.py
@@ -50,7 +50,9 @@
     f32 = jnp.float32
     row_count = features.shape[0]
     head_count = log_decay.shape[0]
-    column_piece = lax.all_gather(features, "head", axis=1, tiled=True)
+    column_piece = jnp.concatenate(
+        lax.all_to_all(jnp.stack([features] * lax.axis_size("head")), "head", 0, 0), axis=1
+    )
     query_sum = jnp.dot(column_piece, w_query, preferred_element_type=f32)
     key_sum = jnp.dot(column_piece, w_key, preferred_element_type=f32)
     value_sum = jnp.dot(column_piece, w_value, preferred_element_type=f32)

time: 225 us -> 233 us (1.036)
  waiting for transfers between devices: 139 us -> 129 us
  starting transfers between devices: 0.3 us -> 8.44 us
  matrix products: 33.9 us -> 39.8 us
  local copies, waits for them, and re-layouts: 3.84 us -> 7.69 us
    all_gather x1 -> x0, waiting for transfers between devices: 36.8 us -> none  [shards(): column_piece = lax.all_gather(features, 'head', axis=1, tiled=True)]
    all_to_all x0 -> x1, waiting for transfers between devices: none -> 27.2 us  [shards(): lax.all_to_all(jnp.stack([features] * lax.axis_size('head')), 'head', 0, 0)]
    all_to_all x0 -> x1, starting transfers between devices: none -> 8.13 us  [shards(): lax.all_to_all(jnp.stack([features] * lax.axis_size('head')), 'head', 0, 0)]
    dot_general x1, matrix products: 1.92 us -> 4.58 us  [shards(): jnp.einsum('tc,dc->td', key_grad_flat, w_key, preferred_element_type=f32)]
  transfers between devices with their start and end apart: 4 -> 4, of which waited for: 4 -> 4; matrix products, arithmetic and copies ran while one was open for 12% -> 11% of each run, Pallas kernels for 0% -> 0%
where the time goes in v1:
time: 233 us; the launch traced here: 232 us
  waiting for transfers between devices  129 us (55%)
  matrix products  39.8 us (17%)
  other arithmetic  17.8 us (8%)
  blocking collectives  14.9 us (6%)
  between operations  14.1 us (6%)
  starting transfers between devices  8.44 us (4%)
  local copies, waits for them, and re-layouts  7.69 us (3%)
    reduce_scatter x1, waiting for transfers between devices, shards(): lax.psum_scatter((summed + jnp.einsum('tc,dc->td', value_grad_flat, w_val...  76 us
    all_to_all x1, waiting for transfers between devices, shards(): lax.all_to_all(jnp.stack([features] * lax.axis_size('head')), 'head', 0, 0)  27.2 us
    all_gather x2, waiting for transfers between devices, prefix(): lax.all_gather(part.astype(kind), axis)  25.8 us
    select_n x16, other arithmetic, lap(): return jax.tree.map(lambda a, b: jnp.where(reached, a, b), new, before)  16.2 us
    unnamed x1, blocking collectives  14.9 us
    all_to_all x1, starting transfers between devices, shards(): lax.all_to_all(jnp.stack([features] * lax.axis_size('head')), 'head', 0, 0)  8.13 us
    dot_general x1, matrix products, shards(): jnp.einsum('tc,dc->td', value_grad_flat, w_value, preferred_element_type=...  6.5 us
    dot_general x1, matrix products, shards(): key_sum = jnp.dot(column_piece, w_key, preferred_element_type=f32)  5.28 us
  transfers between devices with their start and end apart: 4, of which 4 were waited for; matrix products, arithmetic and copies ran while one was open for 11% of the time, Pallas kernels for 0%

profile of v1, /device:TPU:0, one launch (start us, length us, event | category | flops | bytes accessed | tf_op | source)
XLA Modules:
  0.0 232.2 jit_solution(10773799359655721735)
XLA Ops:
  6.5 1.1 copy.40
  7.6 2.0 stack.2
  9.6 8.1 %all-to-all-start = ((bf16[16,256,384]{1,2,0:T(8,128)(2,1)}), bf16[16,256,384]{1,2,0:T(8,128)(2,1)S(1)}, u32[]{:S(2)}, u32[]{:S(2)}) async-start(bf16[16,256,384]{1,2,0:T(8,128)(2,1)} %stack.2), calls=%async_computation | async-start | bytes 6291456 | tf_op jit(solution)/shard_map/all_to_all | solution.py:54
  17.7 0.0 all-gather.8.cloned.1.call-start
  17.8 1.2 reduce-window.6
  19.1 0.1 slice.15
  19.1 0.1 copy.44
  19.3 0.1 copy.45
  19.4 0.1 add_bitcast_fusion
  19.5 0.1 slice.16
  19.5 0.1 copy.77
  19.6 0.6 dynamic-slice
  20.9 0.2 dynamic-update-slice
  21.1 14.9 %all-reduce = bf16[32]{0:T(256)(128)(2,1)S(1)} all-reduce(bf16[32]{0:T(256)(128)(2,1)S(1)} %dynamic-update-slice), channel_id=2, replica_groups=mesh['ctx'=8,'head'=16] {'ctx'}, use_global_device_ids=true, to_apply=%add | all-reduce | flops 32 | bytes 128
  36.1 0.1 reshape.152
  36.1 1.8 copy.72
  38.0 0.1 fusion.44
  38.0 27.2 %all-to-all-done = bf16[16,256,384]{1,2,0:T(8,128)(2,1)S(1)} async-done(((bf16[16,256,384]{1,2,0:T(8,128)(2,1)}), bf16[16,256,384]{1,2,0:T(8,128)(2,1)S(1)}, u32[]{:S(2)}, u32[]{:S(2)}) %all-to-all-start) | async-done | bytes 3145760 | tf_op jit(solution)/shard_map/all_to_all | solution.py:54
  65.2 5.3 %fusion.16 = bf16[32,4,8,128]{3,2,1,0:T(8,128)(2,1)} fusion(bf16[256,6144]{0,1:T(8,128)(2,1)S(1)} %bitcast.156, bf16[6144,512]{1,0:T(8,128)(2,1)} %param.12), kind=kOutput, calls=%fused_computation.33 | convolution fusion | flops 1610743808 | bytes 9699328 | tf_op jit(solution)/shard_map/dot_general | solution.py:57
  70.5 4.6 %fusion.17 = bf16[32,4,8,128]{3,2,1,0:T(8,128)(2,1)S(1)} fusion(bf16[256,6144]{0,1:T(8,128)(2,1)S(1)} %bitcast.157, bf16[6144,512]{1,0:T(8,128)(2,1)} %param.11), kind=kOutput, calls=%fused_computation.34 | convolution fusion | flops 1610743808 | bytes 9699328 | tf_op jit(solution)/shard_map/dot_general | solution.py:56
  75.2 0.7 copy-done.5
  75.9 1.5 convolution_convert_fusion.3
  77.3 0.0 all-gather.8.cloned.1.call-update
  77.4 0.0 all-gather.6.cloned.1.call-start
  77.4 4.6 %fusion.15 = bf16[32,4,8,128]{3,2,1,0:T(8,128)(2,1)S(1)} fusion(bf16[256,6144]{0,1:T(8,128)(2,1)S(1)} %bitcast.158, bf16[6144,512]{1,0:T(8,128)(2,1)} %param.13), kind=kOutput, calls=%fused_computation.32 | convolution fusion | flops 1610743808 | bytes 9699328 | tf_op jit(solution)/shard_map/dot_general | solution.py:58
  82.1 0.7 copy-done.3
  82.7 1.4 convolution_convert_fusion.4
  84.2 1.4 fusion.5
  85.6 1.3 convolution_bitcast_fusion.6
  87.0 1.3 convolution_bitcast_fusion.4
  88.3 1.7 convolution_bitcast_fusion.2
  90.0 0.0 all-gather.6.cloned.1.call-update
  90.0 0.2 reduce-scatter.2.cloned.1.call-start
  90.3 9.3 %all-gather.8.cloned.1.call-done = bf16[32,128,128]{2,1,0:T(8,128)(2,1)} async-done(((bf16[4,128,128]{2,1,0:T(8,128)(2,1)}), bf16[32,128,128]{2,1,0:T(8,128)(2,1)}) %all-gather.8.cloned.1.call-update) | async-done | bytes 1048592 | tf_op jit(solution)/shard_map/all_gather | solution.py:12
  99.5 8.5 %while.31 = (s32[]{:T(128)}, f32[4,128,128]{2,1,0:T(8,128)S(1)}, s32[]{:T(128)}, bf16[8,4,128,128]{3,2,1,0:T(8,128)(2,1)}, bf16[8,4]{1,0:T(8,128)(2,1)S(1)}, /*index=5*/s32[]{:T(128)}, s32[]{:T(128)}, s32[]{:T(128)}, s32[]{:T(128)}) while((s32[]{:T(128)}, f32[4,128,128]{2,1,0:T(8,128)S(1)}, s32[]{:T(128)}, ...), condition=%wide.region_5.6_spmd.clone, body=%wide.region_4.5_spmd.clone.sunk | while | flops 327692 | bytes 655575 | solution.py:30
  99.6 1.0 fusion.67
  100.6 1.0 fusion.67
  101.7 1.0 fusion.67
  102.7 1.0 fusion.67
  103.8 1.0 fusion.67
  104.9 1.0 fusion.67
  105.9 1.0 fusion.67
  107.0 1.0 fusion.67
  108.0 16.5 %all-gather.6.cloned.1.call-done = bf16[32,128,128]{2,1,0:T(8,128)(2,1)} async-done(((bf16[4,128,128]{2,1,0:T(8,128)(2,1)}), bf16[32,128,128]{2,1,0:T(8,128)(2,1)}) %all-gather.6.cloned.1.call-update) | async-done | bytes 1048592 | tf_op jit(solution)/shard_map/all_gather | solution.py:12
  124.5 8.4 %while.30 = (s32[]{:T(128)}, f32[4,128,128]{2,1,0:T(8,128)S(1)}, s32[]{:T(128)}, bf16[8,4]{1,0:T(8,128)(2,1)S(1)}, bf16[8,4,128,128]{3,2,1,0:T(8,128)(2,1)}, /*index=5*/s32[]{:T(128)}, s32[]{:T(128)}) while((s32[]{:T(128)}, f32[4,128,128]{2,1,0:T(8,128)S(1)}, s32[]{:T(128)}, bf16[8,4]{1,0:T(8,128)(2,1)S(1)}, ...), condition=%wide.region_3.4_spmd.clone, body=%wide.region_2.3_spmd.clone.sunk | while | flops 327688 | bytes 655513 | solution.py:30
  124.5 1.0 fusion.66
  125.6 1.0 fusion.66
  126.6 1.0 fusion.66
  127.7 1.0 fusion.66
  128.7 1.0 fusion.66
  129.8 1.0 fusion.66
  130.9 1.0 fusion.66
  131.9 1.0 fusion.66
  132.9 0.3 fusion.12
  133.2 0.2 fusion.13
  133.5 0.0 slice-start
  133.5 0.2 fusion.14
  133.7 0.0 slice-start.1
  133.7 4.8 %fusion.45 = f32[256,6144]{1,0:T(8,128)S(1)} fusion(bf16[256,512]{0,1:T(8,128)(2,1)S(1)} %bitcast.165, bf16[6144,512]{1,0:T(8,128)(2,1)} %param.11), kind=kOutput, calls=%fused_computation.72 | convolution fusion | flops 1610612736 | bytes 12845056 | tf_op jit(solution)/shard_map/tc,dc->td/dot_general | solution.py:113
  138.6 0.0 slice-start.3
  138.6 4.6 %convolution_add_fusion.1 = f32[256,6144]{1,0:T(8,128)} fusion(f32[256,6144]{1,0:T(8,128)S(1)} %fusion.45, bf16[256,512]{0,1:T(8,128)(2,1)S(1)} %bitcast.164, bf16[6144,512]{1,0:T(8,128)(2,1)S(1)} %bitcast.160), kind=kOutput, calls=%fused_computation.7 | convolution fusion | flops 1612185600 | bytes 19136512 | tf_op jit(solution)/shard_map/tc,dc->td/dot_general | solution.py:114
  143.2 6.5 %fusion.2 = bf16[256,6144]{1,0:T(8,128)(2,1)} fusion(f32[256,6144]{1,0:T(8,128)} %convolution_add_fusion.1, bf16[256,512]{0,1:T(8,128)(2,1)S(1)} %bitcast.163, bf16[6144,512]{1,0:T(8,128)(2,1)S(1)} %bitcast.162), kind=kOutput, calls=%fused_computation.8 | convolution fusion | flops 1613758464 | bytes 15990784 | tf_op jit(solution)/shard_map/tc,dc->td/dot_general | solution.py:117
  149.7 0.0 reduce-scatter.2.cloned.1.call-update
  149.7 76.0 %reduce-scatter.2.cloned.1.call-done = bf16[16,6144]{1,0:T(8,128)(2,1)} async-done(((bf16[256,6144]{1,0:T(8,128)(2,1)}), bf16[16,6144]{1,0:T(8,128)(2,1)}) %reduce-scatter.2.cloned.1.call-update) | async-done | bytes 196624 | tf_op jit(solution)/shard_map/reduce_scatter | solution.py:115
  (50 shorter events, 0.3 us)
Async XLA Ops:
  6.5 13.1 %copy-start.9 = (u32[128]{0:T(128)S(1)}, u32[128]{0:T(128)}, u32[]{:S(2)}) copy-start(u32[128]{0:T(128)} %constant.85) | copy-start | bytes 1540
  6.5 11.3 %copy-start.8 = (f32[4,256]{1,0:T(4,128)S(1)}, f32[4,256]{1,0:T(4,128)}, u32[]{:S(2)}) copy-start(f32[4,256]{1,0:T(4,128)} %param.14) | copy-start | bytes 12292
  9.6 55.6 %all-to-all-start = ((bf16[16,256,384]{1,2,0:T(8,128)(2,1)}), bf16[16,256,384]{1,2,0:T(8,128)(2,1)S(1)}, u32[]{:S(2)}, u32[]{:S(2)}) async-start(bf16[16,256,384]{1,2,0:T(8,128)(2,1)} %stack.2), calls=%async_computation | async-start | bytes 6291456 | tf_op jit(solution)/shard_map/all_to_all | solution.py:54
  17.7 81.8 %all-gather.8.cloned.1.call-start = ((), (), s32[]{:S(2)}) async-start(), calls=%async_computation.4 | async-start | bytes 1179648 | tf_op jit(solution)/shard_map/all_gather | solution.py:12
  70.5 5.4 %copy-start.6 = (bf16[256,512]{0,1:T(8,128)(2,1)S(1)}, bf16[256,512]{0,1:T(8,128)(2,1)}, u32[]{:S(2)}) copy-start(bf16[256,512]{0,1:T(8,128)(2,1)} %copy.72) | copy-start | bytes 786436
  75.1 0.7 copy-start.5
  77.4 47.1 %all-gather.6.cloned.1.call-start = ((), (), s32[]{:S(2)}) async-start(), calls=%async_computation.3 | async-start | bytes 1179648 | tf_op jit(solution)/shard_map/all_gather | solution.py:12
  77.4 5.3 %copy-start.1 = (bf16[32,4,8,128]{3,2,1,0:T(8,128)(2,1)S(1)}, bf16[32,4,8,128]{3,2,1,0:T(8,128)(2,1)}, u32[]{:S(2)}) copy-start(bf16[32,4,8,128]{3,2,1,0:T(8,128)(2,1)} %fusion.16) | copy-start | bytes 786436
  82.0 0.7 copy-start.3
  82.1 42.4 %copy-start = (f32[4,128,128]{2,1,0:T(8,128)S(1)}, f32[4,128,128]{2,1,0:T(8,128)}, u32[]{:S(2)}) copy-start(f32[4,128,128]{2,1,0:T(8,128)} %custom-call) | copy-start | bytes 786436
  85.6 47.3 %copy-start.2 = (bf16[32,4,8,128]{3,2,1,0:T(8,128)(2,1)S(1)}, bf16[32,4,8,128]{3,2,1,0:T(8,128)(2,1)}, u32[]{:S(2)}) copy-start(bf16[32,4,8,128]{3,2,1,0:T(8,128)(2,1)} %fusion.16) | copy-start | bytes 786436
  86.9 46.3 %copy-start.4 = (bf16[32,4,8,128]{3,2,1,0:T(8,128)(2,1)S(1)}, bf16[32,4,8,128]{3,2,1,0:T(8,128)(2,1)}, u32[]{:S(2)}) copy-start(bf16[32,4,8,128]{3,2,1,0:T(8,128)(2,1)} %copy-done.3) | copy-start | bytes 786436
  88.3 45.2 %copy-start.7 = (bf16[256,512]{0,1:T(8,128)(2,1)S(1)}, bf16[256,512]{0,1:T(8,128)(2,1)}, u32[]{:S(2)}) copy-start(bf16[256,512]{0,1:T(8,128)(2,1)} %copy.72) | copy-start | bytes 786436
  90.0 135.7 %reduce-scatter.2.cloned.1.call-start = ((), (), s32[]{:S(2)}) async-start(), calls=%async_computation.2 | async-start | bytes 3342336 | tf_op jit(solution)/shard_map/reduce_scatter | solution.py:115
  133.5 5.1 %slice-start = ((s8[6291456]{0:T(1024)(128)(4,1)}), s8[4194304]{0:T(1024)(128)(4,1)S(1)}, s32[]{:S(2)}) async-start(s8[6291456]{0:T(1024)(128)(4,1)} %bitcast.159), calls=%async_computation.5 | async-start | bytes 8388608
  133.7 4.8 %slice-start.1 = ((s8[6291456]{0:T(1024)(128)(4,1)}), s8[2097152]{0:T(1024)(128)(4,1)S(1)}, s32[]{:S(2)}) async-start(s8[6291456]{0:T(1024)(128)(4,1)} %bitcast.159), calls=%async_computation.6 | async-start | bytes 4194304
  133.7 9.4 %slice-start.2 = ((s8[6291456]{0:T(1024)(128)(4,1)}), s8[4194304]{0:T(1024)(128)(4,1)S(1)}, s32[]{:S(2)}) async-start(s8[6291456]{0:T(1024)(128)(4,1)} %bitcast.161), calls=%async_computation.7 | async-start | bytes 8388608
  138.6 4.6 %slice-start.3 = ((s8[6291456]{0:T(1024)(128)(4,1)}), s8[2097152]{0:T(1024)(128)(4,1)S(1)}, s32[]{:S(2)}) async-start(s8[6291456]{0:T(1024)(128)(4,1)} %bitcast.161), calls=%async_computation.8 | async-start | bytes 4194304
Sparse Core Ops, SparseCore 0:
  77.5 22.0 all-gather.7
  101.3 23.1 all-gather.5
  149.8 75.8 reduce-scatter.1
